TPU v7x, 512 devices: a whole 4x8x8 slice. The times are simulated.
512 devices in a mesh: dp: 64 (over y, z_lo, core), mp: 8 (over z_hi, x).
Axes of the slice: x: 4, y: 8, z: 8 (z_hi: 2, z_lo: 4; z = z_hi * 4 + z_lo), core: 2. Of those that a mesh axis runs over, the one named last changes fastest.
Arguments:
- inputs: bfloat16 [131072, 3072], P(('dp', 'mp')), may hold values from -24 to 24
- weight: bfloat16 [3072, 384], P('dp', 'mp'), may hold values from -0.109375 to 0.109375
- d_out: bfloat16 [131072, 128], P(('dp', 'mp')), may hold values from -6 to 6
Outputs:
- grad_inputs: bfloat16 [131072, 3072], P(('dp', 'mp'))
- weight_grad: float32 [3072, 384], P('dp', 'mp')
All inputs are finite; a program needn't handle non-finite values.
Results may differ from a plain program's by a relative error of at most 0.015.
Values may be sent and summed in bfloat16 or wider, within the bound.
A program may use at most 64 MiB of HBM per device.

v0:
```python
import jax
import jax.numpy as jnp
from jax import lax
from jax.sharding import PartitionSpec as P

SEQ = 256


def attend_back(qkv, d_out, images):
    hd = d_out.shape[1]
    blocks = qkv.reshape(images, SEQ, 3 * hd)
    query_rows = blocks[..., :hd]
    key_rows = blocks[..., hd : 2 * hd]
    value_rows = blocks[..., 2 * hd :]
    gradient_list = d_out.reshape(images, SEQ, hd)
    scaling_factor = hd ** (-0.5)
    score_matrix = (
        jnp.einsum("mop,mjp->moj", query_rows, key_rows, preferred_element_type=jnp.float32)
        * scaling_factor
    )
    probs = jax.nn.softmax(score_matrix, axis=-1)
    probabilities_reduced = probs.astype(jnp.bfloat16)
    value_gradient = jnp.einsum(
        "orf,ori->ofi", probabilities_reduced, gradient_list, preferred_element_type=jnp.float32
    )
    probability_gradient = jnp.einsum(
        "mop,mjp->moj", gradient_list, value_rows, preferred_element_type=jnp.float32
    )
    delta = jnp.sum(probs * probability_gradient, axis=-1, keepdims=True)
    score_gradient = (probs * (probability_gradient - delta)).astype(jnp.bfloat16)
    query_gradient = (
        jnp.einsum("xoh,xhw->xow", score_gradient, key_rows, preferred_element_type=jnp.float32)
        * scaling_factor
    )
    key_gradient = (
        jnp.einsum("orf,ori->ofi", score_gradient, query_rows, preferred_element_type=jnp.float32)
        * scaling_factor
    )
    joined = jnp.concatenate([query_gradient, key_gradient, value_gradient], axis=-1)
    return joined.reshape(images * SEQ, 3 * hd).astype(jnp.bfloat16)


def per_device(inputs, weight, d_out):
    columns = lax.all_gather(weight, "mp", axis=1, tiled=True)
    window = lax.all_gather(columns, "dp", axis=0, tiled=True)
    qkv = jnp.dot(inputs, window, preferred_element_type=jnp.float32).astype(jnp.bfloat16)
    grad_qkv = attend_back(qkv, d_out, inputs.shape[0] // SEQ)
    grad_inputs = lax.dot_general(
        grad_qkv, window, (((1,), (1,)), ((), ())), preferred_element_type=jnp.float32
    ).astype(jnp.bfloat16)
    column_sum = lax.psum_scatter(
        lax.dot_general(
            grad_qkv, inputs, (((0,), (0,)), ((), ())), preferred_element_type=jnp.float32
        ).astype(jnp.bfloat16),
        "mp",
        scatter_dimension=0,
        tiled=True,
    ).astype(jnp.float32)
    flipped = column_sum.T
    weight_grad = lax.psum_scatter(flipped, "dp", scatter_dimension=0, tiled=True)
    return (grad_inputs, weight_grad)


def solution(mesh):
    in_specs = (P(("dp", "mp"), None), P("dp", "mp"), P(("dp", "mp"), None))
    out_specs = (P(("dp", "mp"), None), P("dp", "mp"))
    return jax.shard_map(
        per_device, mesh=mesh, in_specs=in_specs, out_specs=out_specs, check_vma=False
    )
```

profile of v0, /device:TPU:1, one launch (start us, length us, event | category | flops | bytes accessed | tf_op | source)
XLA Modules:
  0.0 569.9 jit_solution(3445975094033973786)
XLA Ops:
  7.2 0.0 copy-start
  7.2 0.0 all-gather.2.cloned.1.call-start
  7.2 0.9 copy.8
  8.1 42.3 %all_gather.6 = bf16[48,384]{0,1:T(8,128)(2,1)S(1)} all-gather(bf16[48,48]{0,1:T(8,128)(2,1)S(1)} %copy.8), channel_id=1, replica_groups=mesh['dp'=64,'mp'=8] {'mp'}, dimensions={1}, use_global_device_ids=true | all-gather | bytes 41472 | tf_op jit(solution)/shard_map/all_gather | solution.py:44
  50.4 0.7 copy.9
  51.1 0.0 all-gather.2.cloned.1.call-update
  51.1 0.0 copy-start.1
  51.1 0.0 reduce-scatter.5.cloned.1.call-start
  51.2 126.7 %all-gather.2.cloned.1.call-done = bf16[3072,384]{1,0:T(8,128)(2,1)} async-done(((bf16[48,384]{1,0:T(8,128)(2,1)}), bf16[3072,384]{1,0:T(8,128)(2,1)}) %all-gather.2.cloned.1.call-update) | async-done | bytes 2359312 | tf_op jit(solution)/shard_map/all_gather | solution.py:45
  177.9 0.0 copy-done
  177.9 2.6 fusion
  180.6 0.2 fusion.12
  180.8 0.1 fusion.7
  180.8 0.0 copy-done.1
  180.9 0.2 fusion.3
  181.1 0.2 multiply_reduce_fusion
  181.3 0.1 multiply_convert_fusion
  181.4 0.2 fusion.4
  181.6 0.2 fusion.5
  181.8 2.2 convolution_convert_fusion
  184.0 0.0 reduce-scatter.5.cloned.1.call-update
  184.0 0.0 reduce-scatter.7.cloned.1.call-start
  184.1 100.9 %reduce-scatter.5.cloned.1.call-done = bf16[48,3072]{1,0:T(8,128)(2,1)} async-done(((bf16[384,3072]{1,0:T(8,128)(2,1)}), bf16[48,3072]{1,0:T(8,128)(2,1)}) %reduce-scatter.5.cloned.1.call-update) | async-done | bytes 294928 | tf_op jit(solution)/shard_map/reduce_scatter | solution.py:51
  284.9 1.0 convert_bitcast_fusion
  285.9 1.6 copy.11
  287.6 0.0 reduce-scatter.7.cloned.1.call-update
  287.6 3.8 convolution_convert_fusion.1
  291.4 272.0 %reduce-scatter.7.cloned.1.call-done = f32[48,48]{1,0:T(8,128)} async-done(((f32[3072,48]{1,0:T(8,128)}), f32[48,48]{1,0:T(8,128)}) %reduce-scatter.7.cloned.1.call-update) | async-done | bytes 9232
Async XLA Ops:
  7.2 170.7 %copy-start = (bf16[256,3072]{1,0:T(8,128)(2,1)S(1)}, bf16[256,3072]{1,0:T(8,128)(2,1)}, u32[]{:S(2)}) copy-start(bf16[256,3072]{1,0:T(8,128)(2,1)} %param.3) | copy-start | bytes 4718596
  7.2 170.7 %all-gather.2.cloned.1.call-start = ((), (), s32[]{:S(2)}) async-start(), calls=%async_computation.2 | async-start | bytes 2396160 | tf_op jit(solution)/shard_map/all_gather | solution.py:45
  51.1 129.7 %copy-start.1 = (bf16[256,128]{1,0:T(8,128)(2,1)S(1)}, bf16[256,128]{1,0:T(8,128)(2,1)}, u32[]{:S(2)}) copy-start(bf16[256,128]{1,0:T(8,128)(2,1)} %param.5) | copy-start | bytes 196612
  51.1 233.8 %reduce-scatter.5.cloned.1.call-start = ((), (), s32[]{:S(2)}) async-start(), calls=%async_computation.3 | async-start | bytes 2654208 | tf_op jit(solution)/shard_map/reduce_scatter | solution.py:51
  184.0 379.4 %reduce-scatter.7.cloned.1.call-start = ((), (), s32[]{:S(2)}) async-start(), calls=%async_computation.4 | async-start | bytes 1597440
Sparse Core Ops, SparseCore 0:
  51.3 126.5 all-gather.1
  184.2 100.7 reduce-scatter.4
  288.5 274.8 reduce-scatter.6
where the time goes:
time: 574 us; the launch traced here: 570 us
  waiting for transfers between devices  500 us (87%)
  blocking collectives  42.3 us (7%)
  between operations  13.8 us (2%)
  matrix products  9.76 us (2%)
    unnamed x4, waiting for transfers between devices  272 us
    all_gather x1, waiting for transfers between devices, per_device(): window = lax.all_gather(columns, 'dp', axis=0, tiled=True)  127 us
    reduce_scatter x1, waiting for transfers between devices, per_device(): lax.psum_scatter(lax.dot_general(grad_qkv, inputs, (((0,), (0,)), ((), ()...  101 us
    all_gather x1, blocking collectives, per_device(): columns = lax.all_gather(weight, 'mp', axis=1, tiled=True)  42.3 us
  transfers between devices with their start and end apart: 3, of which 3 were waited for; matrix products, arithmetic and copies ran while one was open for 1% of the time, Pallas kernels for 0%

commit v1 on v0

v1 whole, which is shorter than its diff:
```python
import jax
import jax.numpy as jnp
from jax import lax
from jax.experimental import pallas as pl
from jax.experimental.pallas import tpu as pltpu
from jax.sharding import PartitionSpec as P

MESH = pl.DeviceIdType.MESH
BF = jnp.bfloat16
F32 = jnp.float32

NY, NZL, NC, NM = 8, 4, 2, 8
B = 48
CH = 384
STEPS = (0, 1, 7, 2, 6, 3, 5, 4)


def dot(a, b):
    return jnp.dot(a, b, preferred_element_type=F32)


def dot_nt(a, b):
    return lax.dot_general(a, b, (((1,), (1,)), ((), ())), preferred_element_type=F32)


def dot_tn(a, b):
    return lax.dot_general(a, b, (((0,), (0,)), ((), ())), preferred_element_type=F32)


def attention_back(qkv, d_out):
    hd = 128
    scale = hd**-0.5
    q, k, v = qkv[:, :hd], qkv[:, hd : 2 * hd], qkv[:, 2 * hd :]
    scores = dot_nt(q, k) * scale
    e = jnp.exp(scores - jnp.max(scores, axis=-1, keepdims=True))
    probs = e / jnp.sum(e, axis=-1, keepdims=True)
    grad_v = dot_tn(probs.astype(BF), d_out)
    grad_p = dot_nt(d_out, v)
    delta = jnp.sum(probs * grad_p, axis=-1, keepdims=True)
    grad_s = (probs * (grad_p - delta)).astype(BF)
    grad_q = dot(grad_s, k) * scale
    grad_k = dot_tn(grad_s, q) * scale
    return grad_q.astype(BF), grad_k.astype(BF), grad_v.astype(BF)


def kernel(
    inputs_hbm, weight, d_out, gi_hbm, wg_out,
    inputs, wm, w, acc, g_own, g_other, t_own, t_send, t_other,
    part, rz, s2, ry, sm, rm, gi,
    in_sem, gi_sem, wm_s, wm_r, y_s, y_r, z_s, z_r, c_s, c_r, t_s, t_r, g_s, g_r,
    rz_s, rz_r, ry_s, ry_r, rm_s, rm_r,
):
    dp, mp = lax.axis_index("dp"), lax.axis_index("mp")
    y, zl, c = dp // 8, (dp // 2) % 4, dp % 2
    zh, x = mp // 4, mp % 4
    z = zh * 4 + zl
    oc = 1 - c

    load = pltpu.make_async_copy(inputs_hbm, inputs, in_sem)
    load.start()

    def at(yy, zz, cc):
        return ((yy * 4 + zz % 4) * 2 + cc, (zz // 4) * 4 + x)

    def mp_peer(j):
        return (dp, (mp + j) % 8)

    def y_peer(d, cc):
        return at((y + d) % 8, z, cc)

    far = 2 - 4 * c
    z_steps = (1, -1, far)

    def z_peer(j, sign=1):
        return at(y, (z + sign * z_steps[j] + 8) % 8, c)

    core_peer = at(y, z, oc)

    wm[mp] = jnp.zeros((B, 128), BF)
    wm[mp, :, :B] = weight[...]

    barrier = pltpu.get_barrier_semaphore()
    peers = [mp_peer(j) for j in range(1, 8)]
    peers += [y_peer(d, c) for d in range(1, 8)]
    peers += [y_peer(d, oc) for d in range(0, 8)]
    peers += [at(y, (z + dz + 8) % 8, c) for dz in (1, -1, 2, -2)]
    for peer in peers:
        pl.semaphore_signal(barrier, inc=1, device_id=peer, device_id_type=MESH)
    pl.semaphore_wait(barrier, len(peers))

    def remote(src, dst, ssem, rsem, peer):
        return pltpu.make_async_remote_copy(
            src_ref=src, dst_ref=dst, send_sem=ssem, recv_sem=rsem,
            device_id=peer, device_id_type=MESH,
        )

    def wm_copy(j, slot):
        return remote(wm.at[slot], wm.at[slot], wm_s.at[j], wm_r.at[j], mp_peer(j))

    for j in range(1, 8):
        wm_copy(j, mp).start()

    load.wait()

    def chunk_of(k, half):
        return half * 4 + (k + y) % 4

    def columns(ch):
        return pl.ds(pl.multiple_of(ch * CH, CH), CH)

    for k in range(4):
        t_send[k] = inputs[:, columns(chunk_of(k, oc))].T
    t_copy = remote(t_send, t_other, t_s, t_r, core_peer)
    t_copy.start()

    for j in range(1, 8):
        wm_copy(j, (mp - j + 8) % 8).wait_recv()
    block = jnp.concatenate([wm[m, :, :B] for m in range(NM)], axis=1)
    w[y, zl, c] = block

    def y_copy(d, src_y):
        blk = w.at[src_y, zl, c]
        return remote(blk, blk, y_s.at[d], y_r.at[d], y_peer(d, c))

    def z_copy(k, j, src_y, src_zl):
        blk = w.at[src_y, src_zl, c]
        return remote(blk, blk, z_s.at[k, j], z_r.at[k, j], z_peer(j))

    def c_copy(k, src_y, cc):
        blk = w.at[src_y, :, cc]
        return remote(blk, blk, c_s.at[k], c_r.at[k], core_peer)

    for d in STEPS[1:]:
        y_copy(d, y).start()
    ys = [(y - d + 8) % 8 for d in STEPS]
    zls = [(zl - s + 8) % 4 for s in z_steps]
    for k in range(8):
        if k > 0:
            y_copy(STEPS[k], ys[k]).wait_recv()
        for j in (2, 0, 1):
            z_copy(k, j, ys[k], zl).start()
        if k < 4:
            t_own[k] = inputs[:, columns(chunk_of(k, c))].T

    def multiply(k):
        c_copy(k, ys[k], oc).wait_recv()
        p = dot(inputs[:, columns(ys[k])], w[ys[k]].reshape(CH, CH))
        if k == 0:
            acc[...] = p
        else:
            acc[...] += p

    for k in range(8):
        for j in range(3):
            z_copy(k, j, ys[k], zls[j]).wait_recv()
        c_copy(k, ys[k], c).start()
        if k > 0:
            multiply(k - 1)
    multiply(7)

    gq, gk, gv = attention_back(acc[...].astype(BF), d_out[...])
    g_own[:, :128] = gq
    g_own[:, 128:256] = gk
    g_own[:, 256:] = gv
    g_copy = remote(g_own, g_other, g_s, g_r, core_peer)
    g_copy.start()
    t_copy.wait_recv()
    g_copy.wait_recv()

    def rz_copy(k, j):
        to = (zl + z_steps[j] + 4) % 4
        return remote(
            part.at[k, to], rz.at[j, k], rz_s.at[k, j], rz_r.at[k, j], z_peer(j)
        )

    for k in range(4):
        p = dot(t_own[k], g_own[...]) + dot(t_other[k], g_other[...])
        part[k] = p.astype(BF).reshape(4, 2 * B, CH)
        for j in (2, 0, 1):
            rz_copy(k, j).start()

    def gi_copy(i):
        cols = pl.ds(i * CH, CH)
        return pltpu.make_async_copy(gi.at[:, cols], gi_hbm.at[:, cols], gi_sem.at[i])

    def ry_copy(k, cc):
        return remote(
            s2.at[k, cc], ry.at[y], ry_s.at[k, cc], ry_r.at[y],
            at(chunk_of(k, c), z, cc),
        )

    def is_self(k, cc):
        return jnp.logical_and(chunk_of(k, c) == y, cc == c)

    for k in range(4):
        for i in (2 * k, 2 * k + 1):
            gi[:, i * CH : (i + 1) * CH] = dot_nt(g_own[...], w[i].reshape(CH, CH)).astype(BF)
            gi_copy(i).start()
        for j in range(3):
            rz_copy(k, j).wait_recv()
        total = part[k, zl].astype(F32)
        for j in range(3):
            total += rz[j, k].astype(F32)
        s2[k] = total.astype(BF).reshape(2, B, CH)
        for cc in range(2):
            self_k = is_self(k, cc)

            @pl.when(self_k)
            def _():
                ry[y] = s2[k, cc]

            @pl.when(jnp.logical_not(self_k))
            def _():
                ry_copy(k, cc).start()

    src_core = y // 4
    for i in range(8):

        @pl.when(jnp.logical_not(jnp.logical_and(i == y, src_core == c)))
        def _():
            remote(s2.at[0, 0], ry.at[i], ry_s.at[0, 0], ry_r.at[i], core_peer).wait_recv()

    total = ry[0].astype(F32)
    for i in range(1, 8):
        total += ry[i].astype(F32)

    def rm_copy(j, to, slot):
        return remote(sm.at[to], rm.at[slot], rm_s.at[j], rm_r.at[j], mp_peer(j))

    for m in range(NM):
        sm[m, :, :B] = total[:, m * B : (m + 1) * B].astype(BF)
    for j in range(1, 8):
        rm_copy(j, (mp + j) % 8, mp).start()
    result = sm[mp, :, :B].astype(F32)
    for j in range(1, 8):
        rm_copy(j, 0, (mp - j + 8) % 8).wait_recv()
        result += rm[(mp - j + 8) % 8, :, :B].astype(F32)
    wg_out[...] = result

    for j in range(1, 8):
        wm_copy(j, mp).wait_send()
        y_copy(j, y).wait_send()
        rm_copy(j, 0, mp).wait_send()
    for k in range(8):
        for j in range(3):
            z_copy(k, j, ys[k], zl).wait_send()
        c_copy(k, ys[k], c).wait_send()
        gi_copy(k).wait()
    t_copy.wait_send()
    g_copy.wait_send()
    for k in range(4):
        for j in range(3):
            rz_copy(k, j).wait_send()
        for cc in range(2):

            @pl.when(jnp.logical_not(is_self(k, cc)))
            def _():
                ry_copy(k, cc).wait_send()


def per_device(inputs, weight, d_out):
    vmem, hbm = pl.BlockSpec(memory_space=pltpu.VMEM), pl.BlockSpec(memory_space=pl.ANY)
    dma = pltpu.SemaphoreType.DMA
    tokens, feats = inputs.shape
    return pl.pallas_call(
        kernel,
        out_shape=(
            jax.ShapeDtypeStruct((tokens, feats), BF),
            jax.ShapeDtypeStruct((B, B), F32),
        ),
        in_specs=[hbm, vmem, vmem],
        out_specs=(hbm, vmem),
        scratch_shapes=[
            pltpu.VMEM((tokens, feats), BF),
            pltpu.VMEM((NM, B, 128), BF),
            pltpu.VMEM((NY, NZL, NC, B, CH), BF),
            pltpu.VMEM((tokens, CH), F32),
            pltpu.VMEM((tokens, CH), BF),
            pltpu.VMEM((tokens, CH), BF),
            pltpu.VMEM((4, CH, tokens), BF),
            pltpu.VMEM((4, CH, tokens), BF),
            pltpu.VMEM((4, CH, tokens), BF),
            pltpu.VMEM((4, 4, 2 * B, CH), BF),
            pltpu.VMEM((3, 4, 2 * B, CH), BF),
            pltpu.VMEM((4, NC, B, CH), BF),
            pltpu.VMEM((NY, B, CH), BF),
            pltpu.VMEM((NM, B, 128), BF),
            pltpu.VMEM((NM, B, 128), BF),
            pltpu.VMEM((tokens, feats), BF),
            dma,
            dma((8,)),
            dma((8,)), dma((8,)),
            dma((8,)), dma((8,)),
            dma((8, 3)), dma((8, 3)),
            dma((8,)), dma((8,)),
            dma, dma,
            dma, dma,
            dma((4, 3)), dma((4, 3)),
            dma((4, 2)), dma((8,)),
            dma((8,)), dma((8,)),
        ],
        compiler_params=pltpu.CompilerParams(
            collective_id=0, has_side_effects=True, vmem_limit_bytes=40 << 20
        ),
        name="attention_head_back",
    )(inputs, weight, d_out)


def solution(mesh):
    in_specs = (P(("dp", "mp"), None), P("dp", "mp"), P(("dp", "mp"), None))
    out_specs = (P(("dp", "mp"), None), P("dp", "mp"))
    return jax.shard_map(
        per_device, mesh=mesh, in_specs=in_specs, out_specs=out_specs, check_vma=False
    )
```

time: 574 us -> 74.8 us (0.13)
  waiting for transfers between devices: 500 us -> 0 us
  Pallas kernels: 0 us -> 69.2 us
  blocking collectives: 42.3 us -> 0 us
  between operations: 13.8 us -> 0.65 us
  matrix products: 9.76 us -> 0 us
    unnamed x4 -> x0, waiting for transfers between devices: 272 us -> none
    all_gather x1 -> x0, waiting for transfers between devices: 127 us -> none  [per_device(): window = lax.all_gather(columns, 'dp', axis=0, tiled=True)]
    reduce_scatter x1 -> x0, waiting for transfers between devices: 101 us -> none  [per_device(): lax.psum_scatter(lax.dot_general(grad_qkv, inputs, (((0,), (0,)), ((), ()...]
    pallas_call x0 -> x1, Pallas kernels: none -> 69.2 us  [per_device(): pl.pallas_call(kernel, out_shape=(jax.ShapeDtypeStruct((tokens, feats), B...]
    all_gather x1 -> x0, blocking collectives: 42.3 us -> none  [per_device(): columns = lax.all_gather(weight, 'mp', axis=1, tiled=True)]
    dot_general x8 -> x0, matrix products: 9.76 us -> none  [the longest x1 3.83 us: per_device(): lax.dot_general(grad_qkv, window, (((1,), (1,)), ((), ())), preferred_ele...]
  transfers between devices with their start and end apart: 3 -> 0, of which waited for: 3 -> 0; matrix products, arithmetic and copies ran while one was open for 1% -> 0% of each run, Pallas kernels for 0% -> 0%
where the time goes in v1:
time: 74.8 us; the launch traced here: 74.5 us
  Pallas kernels  69.2 us (93%)
  local copies, waits for them, and re-layouts  4.7 us (6%)
    pallas_call x1, Pallas kernels, per_device(): pl.pallas_call(kernel, out_shape=(jax.ShapeDtypeStruct((tokens, feats), B...  69.2 us
    unnamed x8, local copies, waits for them, and re-layouts  4.7 us

profile of v1, /device:TPU:1, one launch (start us, length us, event | category | flops | bytes accessed | tf_op | source)
XLA Modules:
  0.0 74.5 jit_solution(1121764625987534244)
XLA Ops:
  0.6 0.0 copy-start
  0.6 1.4 %copy-done = bf16[256,3072]{1,0:T(8,128)(2,1)S(1)} copy-done((bf16[256,3072]{1,0:T(8,128)(2,1)S(1)}, bf16[256,3072]{1,0:T(8,128)(2,1)}, u32[]{:S(2)}) %copy-start) | copy-done | bytes 1572888
  2.0 0.0 copy-start.1
  2.0 0.8 %copy-done.1 = bf16[256,128]{1,0:T(8,128)(2,1)S(1)} copy-done((bf16[256,128]{1,0:T(8,128)(2,1)S(1)}, bf16[256,128]{1,0:T(8,128)(2,1)}, u32[]{:S(2)}) %copy-start.1) | copy-done | bytes 65560
  2.9 0.0 copy-start.2
  2.9 0.7 copy-done.2
  3.6 69.2 %attention_head_back.1 = (bf16[256,3072]{1,0:T(8,128)(2,1)S(1)}, f32[48,48]{1,0:T(8,128)S(1)}) custom-call(bf16[256,3072]{1,0:T(8,128)(2,1)S(1)} %copy-done, bf16[48,48]{1,0:T(8,128)(2,1)S(1)} %copy-done.2, bf16[256,128]{1,0:T(8,128)(2,1)S(1)} %copy-done.1), custom_call_target="tpu_custom_call" | custom-call | tf_op jit(solution)/shard_map/attention_head_back/pallas_call | solution.py:265
  72.8 1.1 %copy.7 = bf16[256,3072]{1,0:T(8,128)(2,1)} copy(bf16[256,3072]{1,0:T(8,128)(2,1)S(1)} %get-tuple-element.4) | data formatting | bytes 3145728
  73.9 0.6 copy.8
Async XLA Ops:
  0.6 1.4 %copy-start = (bf16[256,3072]{1,0:T(8,128)(2,1)S(1)}, bf16[256,3072]{1,0:T(8,128)(2,1)}, u32[]{:S(2)}) copy-start(bf16[256,3072]{1,0:T(8,128)(2,1)} %inputs_hbm.1) | copy-start | bytes 4718596
  2.0 0.8 %copy-start.1 = (bf16[256,128]{1,0:T(8,128)(2,1)S(1)}, bf16[256,128]{1,0:T(8,128)(2,1)}, u32[]{:S(2)}) copy-start(bf16[256,128]{1,0:T(8,128)(2,1)} %d_out.1) | copy-start | bytes 196612
  2.9 0.7 copy-start.2

commit v2 on v1

--- a/solution.py
+++ b/solution.py
@@ -44,11 +44,11 @@
 
 
 def kernel(
-    inputs_hbm, weight, d_out, gi_hbm, wg_out,
-    inputs, wm, w, acc, g_own, g_other, t_own, t_send, t_other,
-    part, rz, s2, ry, sm, rm, gi,
-    in_sem, gi_sem, wm_s, wm_r, y_s, y_r, z_s, z_r, c_s, c_r, t_s, t_r, g_s, g_r,
-    rz_s, rz_r, ry_s, ry_r, rm_s, rm_r,
+    inputs_hbm, weight_hbm, d_out_hbm, gi, wg_out,
+    inputs, weight, d_out, wm, w, acc, g_own, g_other, t_own, t_send, t_other,
+    part, rx, sx, rz, s2, ry, sm, rm,
+    in_sem, wm_s, wm_r, y_s, y_r, z_s, z_r, x_s, x_r, c_s, c_r, t_s, t_r, g_s, g_r,
+    rx_s, rx_r, rz_s, rz_r, ry_s, ry_r, rm_s, rm_r,
 ):
     dp, mp = lax.axis_index("dp"), lax.axis_index("mp")
     y, zl, c = dp // 8, (dp // 2) % 4, dp % 2
@@ -56,8 +56,12 @@
     z = zh * 4 + zl
     oc = 1 - c
 
-    load = pltpu.make_async_copy(inputs_hbm, inputs, in_sem)
+    load_w = pltpu.make_async_copy(weight_hbm, weight, in_sem.at[0])
+    load_w.start()
+    load = pltpu.make_async_copy(inputs_hbm, inputs, in_sem.at[1])
     load.start()
+    load_d = pltpu.make_async_copy(d_out_hbm, d_out, in_sem.at[2])
+    load_d.start()
 
     def at(yy, zz, cc):
         return ((yy * 4 + zz % 4) * 2 + cc, (zz // 4) * 4 + x)
@@ -74,10 +78,10 @@
     def z_peer(j, sign=1):
         return at(y, (z + sign * z_steps[j] + 8) % 8, c)
 
+    def x_peer(p):
+        return (dp, zh * 4 + (x + p) % 4)
+
     core_peer = at(y, z, oc)
-
-    wm[mp] = jnp.zeros((B, 128), BF)
-    wm[mp, :, :B] = weight[...]
 
     barrier = pltpu.get_barrier_semaphore()
     peers = [mp_peer(j) for j in range(1, 8)]
@@ -86,6 +90,9 @@
     peers += [at(y, (z + dz + 8) % 8, c) for dz in (1, -1, 2, -2)]
     for peer in peers:
         pl.semaphore_signal(barrier, inc=1, device_id=peer, device_id_type=MESH)
+    load_w.wait()
+    wm[mp] = jnp.zeros((B, 128), BF)
+    wm[mp, :, :B] = weight[...]
     pl.semaphore_wait(barrier, len(peers))
 
     def remote(src, dst, ssem, rsem, peer):
@@ -101,6 +108,7 @@
         wm_copy(j, mp).start()
 
     load.wait()
+    load_d.wait()
 
     def chunk_of(k, half):
         return half * 4 + (k + y) % 4
@@ -130,32 +138,69 @@
         blk = w.at[src_y, :, cc]
         return remote(blk, blk, c_s.at[k], c_r.at[k], core_peer)
 
+    def x_copy(p, j, src_y, src_zl):
+        blk = w.at[src_y, src_zl, c]
+        return remote(blk, blk, x_s.at[p, j], x_r.at[p, j], x_peer(p))
+
     for d in STEPS[1:]:
         y_copy(d, y).start()
     ys = [(y - d + 8) % 8 for d in STEPS]
     zls = [(zl - s + 8) % 4 for s in z_steps]
-    for k in range(8):
-        if k > 0:
+
+    def shared_y(xx):
+        return (y - jnp.where(xx == 2, 7, jnp.where(xx == 3, 2, xx)) + 8) % 8
+
+    my_shared = shared_y(x)
+    for k in range(1, 4):
+
+        @pl.when(x == k)
+        def _():
             y_copy(STEPS[k], ys[k]).wait_recv()
+
+    for j in (2, 0, 1):
+        z_copy(0, j, my_shared, zl).start()
+    for k in range(4, 8):
+        y_copy(STEPS[k], ys[k]).wait_recv()
         for j in (2, 0, 1):
             z_copy(k, j, ys[k], zl).start()
-        if k < 4:
-            t_own[k] = inputs[:, columns(chunk_of(k, c))].T
-
-    def multiply(k):
-        c_copy(k, ys[k], oc).wait_recv()
-        p = dot(inputs[:, columns(ys[k])], w[ys[k]].reshape(CH, CH))
-        if k == 0:
+    for k in range(1, 4):
+
+        @pl.when(x != k)
+        def _():
+            y_copy(STEPS[k], ys[k]).wait_recv()
+
+    for j in (0, 1, 2):
+        z_copy(0, j, my_shared, zls[j]).wait_recv()
+        for p in (2, 1, 3):
+            x_copy(p, j, my_shared, zls[j]).start()
+    for k in range(4):
+        t_own[k] = inputs[:, columns(chunk_of(k, c))].T
+
+    x_from = [(x - p + 4) % 4 for p in (1, 2, 3)]
+    order = [(x, my_shared), (4, ys[4]), (5, ys[5])]
+    order += [(xx, shared_y(xx)) for xx in x_from]
+    order += [(6, ys[6]), (7, ys[7])]
+
+    def multiply(n):
+        k, yy = order[n]
+        c_copy(k, yy, oc).wait_recv()
+        p = dot(inputs[:, columns(yy)], w[yy].reshape(CH, CH))
+        if n == 0:
             acc[...] = p
         else:
             acc[...] += p
 
-    for k in range(8):
-        for j in range(3):
-            z_copy(k, j, ys[k], zls[j]).wait_recv()
-        c_copy(k, ys[k], c).start()
-        if k > 0:
-            multiply(k - 1)
+    for n in range(8):
+        k, yy = order[n]
+        if n in (1, 2, 6, 7):
+            for j in range(3):
+                z_copy(k, j, yy, zls[j]).wait_recv()
+        if n in (3, 4, 5):
+            for j in range(3):
+                x_copy(n - 2, j, yy, zls[j]).wait_recv()
+        c_copy(k, yy, c).start()
+        if n > 0:
+            multiply(n - 1)
     multiply(7)
 
     gq, gk, gv = attention_back(acc[...].astype(BF), d_out[...])
@@ -167,21 +212,19 @@
     t_copy.wait_recv()
     g_copy.wait_recv()
 
+    dest_zl = [(zl + s + 4) % 4 for s in z_steps]
+    owner = x // 2 == c
+    mine = x % 2
+
+    def rx_copy(k, p, j):
+        to = dest_zl[j]
+        return remote(
+            part.at[k, to], rx.at[p, j], rx_s.at[k, j], rx_r.at[p, j], x_peer(p)
+        )
+
     def rz_copy(k, j):
-        to = (zl + z_steps[j] + 4) % 4
-        return remote(
-            part.at[k, to], rz.at[j, k], rz_s.at[k, j], rz_r.at[k, j], z_peer(j)
-        )
-
-    for k in range(4):
-        p = dot(t_own[k], g_own[...]) + dot(t_other[k], g_other[...])
-        part[k] = p.astype(BF).reshape(4, 2 * B, CH)
-        for j in (2, 0, 1):
-            rz_copy(k, j).start()
-
-    def gi_copy(i):
-        cols = pl.ds(i * CH, CH)
-        return pltpu.make_async_copy(gi.at[:, cols], gi_hbm.at[:, cols], gi_sem.at[i])
+        src = sx.at[j] if k == 0 else part.at[k, dest_zl[j]]
+        return remote(src, rz.at[j, k], rz_s.at[k, j], rz_r.at[k, j], z_peer(j))
 
     def ry_copy(k, cc):
         return remote(
@@ -192,16 +235,8 @@
     def is_self(k, cc):
         return jnp.logical_and(chunk_of(k, c) == y, cc == c)
 
-    for k in range(4):
-        for i in (2 * k, 2 * k + 1):
-            gi[:, i * CH : (i + 1) * CH] = dot_nt(g_own[...], w[i].reshape(CH, CH)).astype(BF)
-            gi_copy(i).start()
-        for j in range(3):
-            rz_copy(k, j).wait_recv()
-        total = part[k, zl].astype(F32)
-        for j in range(3):
-            total += rz[j, k].astype(F32)
-        s2[k] = total.astype(BF).reshape(2, B, CH)
+    def send_y(k, total):
+        s2[k] = total.reshape(2, B, CH)
         for cc in range(2):
             self_k = is_self(k, cc)
 
@@ -212,6 +247,62 @@
             @pl.when(jnp.logical_not(self_k))
             def _():
                 ry_copy(k, cc).start()
+
+    for k in range(4):
+        p = dot(t_own[k], g_own[...]) + dot(t_other[k], g_other[...])
+        part[k] = p.astype(BF).reshape(4, 2 * B, CH)
+        if k < 2:
+            to_owner = (2 * c + k - x + 4) % 4
+
+            @pl.when(to_owner != 0)
+            def _():
+                for j in (2, 0, 1):
+                    rx_copy(k, to_owner, j).start()
+        else:
+            for j in (2, 0, 1):
+                rz_copy(k, j).start()
+    for k in range(2):
+
+        @pl.when(x != 2 * c + k)
+        def _():
+            send_y(k, part[k, zl])
+
+    def grad_inputs(i):
+        gi[:, i * CH : (i + 1) * CH] = dot_nt(g_own[...], w[i].reshape(CH, CH)).astype(BF)
+
+    for i in range(4):
+        grad_inputs(i)
+    for n, j in enumerate((2, 0, 1)):
+
+        @pl.when(owner)
+        def _():
+            total = part[mine, dest_zl[j]].astype(F32)
+            for p in (1, 2, 3):
+                rx_copy(0, p, j).wait_recv()
+                total += rx[p, j].astype(F32)
+            sx[j] = total.astype(BF)
+            rz_copy(0, j).start()
+
+        grad_inputs(4 + n)
+    grad_inputs(7)
+
+    def from_z(k, total):
+        for j in range(3):
+            rz_copy(k, j).wait_recv()
+            total += rz[j, k].astype(F32)
+        return total.astype(BF)
+
+    for k in (2, 3):
+        send_y(k, from_z(k, part[k, zl].astype(F32)))
+
+    @pl.when(owner)
+    def _():
+        total = from_z(0, part[mine, zl].astype(F32))
+        for k in range(2):
+
+            @pl.when(mine == k)
+            def _():
+                send_y(k, total)
 
     src_core = y // 4
     for i in range(8):
@@ -241,16 +332,31 @@
         wm_copy(j, mp).wait_send()
         y_copy(j, y).wait_send()
         rm_copy(j, 0, mp).wait_send()
+    for j in range(3):
+        for k in (0, 4, 5, 6, 7):
+            z_copy(k, j, ys[k], zl).wait_send()
+        for p in (1, 2, 3):
+            x_copy(p, j, y, zl).wait_send()
+        for k in (2, 3):
+            rz_copy(k, j).wait_send()
     for k in range(8):
-        for j in range(3):
-            z_copy(k, j, ys[k], zl).wait_send()
         c_copy(k, ys[k], c).wait_send()
-        gi_copy(k).wait()
     t_copy.wait_send()
     g_copy.wait_send()
+
+    @pl.when(owner)
+    def _():
+        for j in range(3):
+            rz_copy(0, j).wait_send()
+
+    for k in range(2):
+
+        @pl.when(x != 2 * c + k)
+        def _():
+            for j in range(3):
+                rx_copy(k, 1, j).wait_send()
+
     for k in range(4):
-        for j in range(3):
-            rz_copy(k, j).wait_send()
         for cc in range(2):
 
             @pl.when(jnp.logical_not(is_self(k, cc)))
@@ -259,7 +365,7 @@
 
 
 def per_device(inputs, weight, d_out):
-    vmem, hbm = pl.BlockSpec(memory_space=pltpu.VMEM), pl.BlockSpec(memory_space=pl.ANY)
+    vmem, hbm = pl.BlockSpec(memory_space=pltpu.VMEM), pl.BlockSpec(memory_space=pltpu.HBM)
     dma = pltpu.SemaphoreType.DMA
     tokens, feats = inputs.shape
     return pl.pallas_call(
@@ -268,10 +374,12 @@
             jax.ShapeDtypeStruct((tokens, feats), BF),
             jax.ShapeDtypeStruct((B, B), F32),
         ),
-        in_specs=[hbm, vmem, vmem],
-        out_specs=(hbm, vmem),
+        in_specs=[hbm, hbm, hbm],
+        out_specs=(vmem, vmem),
         scratch_shapes=[
             pltpu.VMEM((tokens, feats), BF),
+            pltpu.VMEM((B, B), BF),
+            pltpu.VMEM((tokens, 128), BF),
             pltpu.VMEM((NM, B, 128), BF),
             pltpu.VMEM((NY, NZL, NC, B, CH), BF),
             pltpu.VMEM((tokens, CH), F32),
@@ -281,26 +389,28 @@
             pltpu.VMEM((4, CH, tokens), BF),
             pltpu.VMEM((4, CH, tokens), BF),
             pltpu.VMEM((4, 4, 2 * B, CH), BF),
+            pltpu.VMEM((4, 3, 2 * B, CH), BF),
+            pltpu.VMEM((3, 2 * B, CH), BF),
             pltpu.VMEM((3, 4, 2 * B, CH), BF),
             pltpu.VMEM((4, NC, B, CH), BF),
             pltpu.VMEM((NY, B, CH), BF),
             pltpu.VMEM((NM, B, 128), BF),
             pltpu.VMEM((NM, B, 128), BF),
-            pltpu.VMEM((tokens, feats), BF),
-            dma,
-            dma((8,)),
+            dma((3,)),
             dma((8,)), dma((8,)),
             dma((8,)), dma((8,)),
             dma((8, 3)), dma((8, 3)),
+            dma((4, 3)), dma((4, 3)),
             dma((8,)), dma((8,)),
             dma, dma,
             dma, dma,
+            dma((2, 3)), dma((4, 3)),
             dma((4, 3)), dma((4, 3)),
             dma((4, 2)), dma((8,)),
             dma((8,)), dma((8,)),
         ],
         compiler_params=pltpu.CompilerParams(
-            collective_id=0, has_side_effects=True, vmem_limit_bytes=40 << 20
+            collective_id=0, has_side_effects=True, vmem_limit_bytes=54_500_000
         ),
         name="attention_head_back",
     )(inputs, weight, d_out)

time: 74.8 us -> 72.8 us (0.973)
  local copies, waits for them, and re-layouts: 4.7 us -> 3.29 us
    unnamed x8 -> x6, local copies, waits for them, and re-layouts: 4.7 us -> 3.29 us
where the time goes in v2:
time: 72.8 us; the launch traced here: 72.5 us
  Pallas kernels  68.6 us (94%)
  local copies, waits for them, and re-layouts  3.29 us (5%)
    pallas_call x1, Pallas kernels, per_device(): pl.pallas_call(kernel, out_shape=(jax.ShapeDtypeStruct((tokens, feats), B...  68.6 us
    unnamed x6, local copies, waits for them, and re-layouts  3.29 us

profile of v2, /device:TPU:1, one launch (start us, length us, event | category | flops | bytes accessed | tf_op | source)
XLA Modules:
  0.0 72.5 jit_solution(4642792552541965849)
XLA Ops:
  0.6 0.0 copy-start
  0.6 0.8 %copy-done = bf16[256,128]{1,0:T(8,128)(2,1)S(1)} copy-done((bf16[256,128]{1,0:T(8,128)(2,1)S(1)}, bf16[256,128]{1,0:T(8,128)(2,1)}, u32[]{:S(2)}) %copy-start) | copy-done | bytes 65560
  1.5 0.0 copy-start.1
  1.5 0.7 copy-done.1
  2.2 68.6 %attention_head_back.1 = (bf16[256,3072]{1,0:T(8,128)(2,1)S(1)}, f32[48,48]{1,0:T(8,128)S(1)}) custom-call(bf16[256,3072]{1,0:T(8,128)(2,1)} %inputs_hbm.1, bf16[48,48]{1,0:T(8,128)(2,1)S(1)} %copy-done.1, bf16[256,128]{1,0:T(8,128)(2,1)S(1)} %copy-done), custom_call_target="tpu_custom_call" | custom-call | tf_op jit(solution)/shard_map/attention_head_back/pallas_call | solution.py:371
  70.8 1.1 %copy.7 = bf16[256,3072]{1,0:T(8,128)(2,1)} copy(bf16[256,3072]{1,0:T(8,128)(2,1)S(1)} %get-tuple-element.4) | data formatting | bytes 3145728
  71.9 0.6 copy.8
Async XLA Ops:
  0.6 0.8 %copy-start = (bf16[256,128]{1,0:T(8,128)(2,1)S(1)}, bf16[256,128]{1,0:T(8,128)(2,1)}, u32[]{:S(2)}) copy-start(bf16[256,128]{1,0:T(8,128)(2,1)} %d_out_hbm.1) | copy-start | bytes 196612
  1.5 0.7 copy-start.1

commit v3 on v2

--- a/solution.py
+++ b/solution.py
@@ -11,6 +11,7 @@
 
 NY, NZL, NC, NM = 8, 4, 2, 8
 B = 48
+PK = 32
 CH = 384
 STEPS = (0, 1, 7, 2, 6, 3, 5, 4)
 
@@ -25,6 +26,12 @@
 
 def dot_tn(a, b):
     return lax.dot_general(a, b, (((0,), (0,)), ((), ())), preferred_element_type=F32)
+
+
+def packed(a):
+    low = jnp.concatenate([a[PK:], jnp.zeros((2 * PK - B, B), a.dtype)], axis=0)
+    pad = jnp.zeros((PK, 128 - 2 * B), a.dtype)
+    return jnp.concatenate([a[:PK], low, pad], axis=1)
 
 
 def attention_back(qkv, d_out):
@@ -91,8 +98,7 @@
     for peer in peers:
         pl.semaphore_signal(barrier, inc=1, device_id=peer, device_id_type=MESH)
     load_w.wait()
-    wm[mp] = jnp.zeros((B, 128), BF)
-    wm[mp, :, :B] = weight[...]
+    wm[mp] = packed(weight[...])
     pl.semaphore_wait(barrier, len(peers))
 
     def remote(src, dst, ssem, rsem, peer):
@@ -104,7 +110,7 @@
     def wm_copy(j, slot):
         return remote(wm.at[slot], wm.at[slot], wm_s.at[j], wm_r.at[j], mp_peer(j))
 
-    for j in range(1, 8):
+    for j in (6, 5, 7, 4, 2, 1, 3):
         wm_copy(j, mp).start()
 
     load.wait()
@@ -123,8 +129,8 @@
 
     for j in range(1, 8):
         wm_copy(j, (mp - j + 8) % 8).wait_recv()
-    block = jnp.concatenate([wm[m, :, :B] for m in range(NM)], axis=1)
-    w[y, zl, c] = block
+    w[y, zl, c, :PK] = jnp.concatenate([wm[m, :, :B] for m in range(NM)], axis=1)
+    w[y, zl, c, PK:] = jnp.concatenate([wm[m, : B - PK, B : 2 * B] for m in range(NM)], axis=1)
 
     def y_copy(d, src_y):
         blk = w.at[src_y, zl, c]
@@ -142,8 +148,14 @@
         blk = w.at[src_y, src_zl, c]
         return remote(blk, blk, x_s.at[p, j], x_r.at[p, j], x_peer(p))
 
-    for d in STEPS[1:]:
-        y_copy(d, y).start()
+    for k in range(1, 4):
+
+        @pl.when(x == k)
+        def _():
+            y_copy(STEPS[k], y).start()
+
+    for k in range(4, 8):
+        y_copy(STEPS[k], y).start()
     ys = [(y - d + 8) % 8 for d in STEPS]
     zls = [(zl - s + 8) % 4 for s in z_steps]
 
@@ -156,6 +168,8 @@
         @pl.when(x == k)
         def _():
             y_copy(STEPS[k], ys[k]).wait_recv()
+            for p in (2, 1, 3):
+                x_copy(p, 3, my_shared, zl).start()
 
     for j in (2, 0, 1):
         z_copy(0, j, my_shared, zl).start()
@@ -163,12 +177,6 @@
         y_copy(STEPS[k], ys[k]).wait_recv()
         for j in (2, 0, 1):
             z_copy(k, j, ys[k], zl).start()
-    for k in range(1, 4):
-
-        @pl.when(x != k)
-        def _():
-            y_copy(STEPS[k], ys[k]).wait_recv()
-
     for j in (0, 1, 2):
         z_copy(0, j, my_shared, zls[j]).wait_recv()
         for p in (2, 1, 3):
@@ -198,10 +206,16 @@
         if n in (3, 4, 5):
             for j in range(3):
                 x_copy(n - 2, j, yy, zls[j]).wait_recv()
+
+            @pl.when(x_from[n - 3] != 0)
+            def _():
+                x_copy(n - 2, 3, yy, zl).wait_recv()
+
         c_copy(k, yy, c).start()
-        if n > 0:
-            multiply(n - 1)
-    multiply(7)
+        if n > 3:
+            multiply(n - 4)
+    for n in range(4, 8):
+        multiply(n)
 
     gq, gk, gv = attention_back(acc[...].astype(BF), d_out[...])
     g_own[:, :128] = gq
@@ -319,18 +333,18 @@
         return remote(sm.at[to], rm.at[slot], rm_s.at[j], rm_r.at[j], mp_peer(j))
 
     for m in range(NM):
-        sm[m, :, :B] = total[:, m * B : (m + 1) * B].astype(BF)
-    for j in range(1, 8):
+        sm[m] = packed(total[:, m * B : (m + 1) * B].astype(BF))
+    for j in (6, 5, 7, 4, 2, 1, 3):
         rm_copy(j, (mp + j) % 8, mp).start()
-    result = sm[mp, :, :B].astype(F32)
+    result = sm[mp].astype(F32)
     for j in range(1, 8):
         rm_copy(j, 0, (mp - j + 8) % 8).wait_recv()
-        result += rm[(mp - j + 8) % 8, :, :B].astype(F32)
-    wg_out[...] = result
+        result += rm[(mp - j + 8) % 8].astype(F32)
+    wg_out[:PK] = result[:, :B]
+    wg_out[PK:] = result[: B - PK, B : 2 * B]
 
     for j in range(1, 8):
         wm_copy(j, mp).wait_send()
-        y_copy(j, y).wait_send()
         rm_copy(j, 0, mp).wait_send()
     for j in range(3):
         for k in (0, 4, 5, 6, 7):
@@ -339,6 +353,16 @@
             x_copy(p, j, y, zl).wait_send()
         for k in (2, 3):
             rz_copy(k, j).wait_send()
+    for k in range(1, 4):
+
+        @pl.when(x == k)
+        def _():
+            y_copy(STEPS[k], y).wait_send()
+            for p in (1, 2, 3):
+                x_copy(p, 3, y, zl).wait_send()
+
+    for k in range(4, 8):
+        y_copy(STEPS[k], y).wait_send()
     for k in range(8):
         c_copy(k, ys[k], c).wait_send()
     t_copy.wait_send()
@@ -368,6 +392,9 @@
     vmem, hbm = pl.BlockSpec(memory_space=pltpu.VMEM), pl.BlockSpec(memory_space=pltpu.HBM)
     dma = pltpu.SemaphoreType.DMA
     tokens, feats = inputs.shape
+    inputs, weight, d_out = (
+        pltpu.with_memory_space_constraint(a, pltpu.HBM) for a in (inputs, weight, d_out)
+    )
     return pl.pallas_call(
         kernel,
         out_shape=(
@@ -380,7 +407,7 @@
             pltpu.VMEM((tokens, feats), BF),
             pltpu.VMEM((B, B), BF),
             pltpu.VMEM((tokens, 128), BF),
-            pltpu.VMEM((NM, B, 128), BF),
+            pltpu.VMEM((NM, PK, 128), BF),
             pltpu.VMEM((NY, NZL, NC, B, CH), BF),
             pltpu.VMEM((tokens, CH), F32),
             pltpu.VMEM((tokens, CH), BF),
@@ -394,13 +421,13 @@
             pltpu.VMEM((3, 4, 2 * B, CH), BF),
             pltpu.VMEM((4, NC, B, CH), BF),
             pltpu.VMEM((NY, B, CH), BF),
-            pltpu.VMEM((NM, B, 128), BF),
-            pltpu.VMEM((NM, B, 128), BF),
+            pltpu.VMEM((NM, PK, 128), BF),
+            pltpu.VMEM((NM, PK, 128), BF),
             dma((3,)),
             dma((8,)), dma((8,)),
             dma((8,)), dma((8,)),
             dma((8, 3)), dma((8, 3)),
-            dma((4, 3)), dma((4, 3)),
+            dma((4, 4)), dma((4, 4)),
             dma((8,)), dma((8,)),
             dma, dma,
             dma, dma,

time: 72.8 us -> 67.6 us (0.929)
  Pallas kernels: 68.6 us -> 64.8 us
  local copies, waits for them, and re-layouts: 3.29 us -> 1.75 us
    pallas_call x1, Pallas kernels: 68.6 us -> 64.8 us  [per_device(): pl.pallas_call(kernel, out_shape=(jax.ShapeDtypeStruct((tokens, feats), B...]
    unnamed x6 -> x2, local copies, waits for them, and re-layouts: 3.29 us -> 1.75 us
where the time goes in v3:
time: 67.6 us; the launch traced here: 67.2 us
  Pallas kernels  64.8 us (96%)
  local copies, waits for them, and re-layouts  1.75 us (3%)
    pallas_call x1, Pallas kernels, per_device(): pl.pallas_call(kernel, out_shape=(jax.ShapeDtypeStruct((tokens, feats), B...  64.8 us
    unnamed x2, local copies, waits for them, and re-layouts  1.75 us

profile of v3, /device:TPU:1, one launch (start us, length us, event | category | flops | bytes accessed | tf_op | source)
XLA Modules:
  0.0 67.2 jit_solution(4554383904475626750)
XLA Ops:
  0.6 64.8 %attention_head_back.1 = (bf16[256,3072]{1,0:T(8,128)(2,1)S(1)}, f32[48,48]{1,0:T(8,128)S(1)}) custom-call(bf16[256,3072]{1,0:T(8,128)(2,1)} %inputs_hbm.1, bf16[48,48]{1,0:T(8,128)(2,1)} %weight_hbm.1, bf16[256,128]{1,0:T(8,128)(2,1)} %d_out_hbm.1), custom_call_target="tpu_custom_call" | custom-call | tf_op jit(solution)/shard_map/attention_head_back/pallas_call | solution.py:398
  65.4 1.1 %copy.7 = bf16[256,3072]{1,0:T(8,128)(2,1)} copy(bf16[256,3072]{1,0:T(8,128)(2,1)S(1)} %get-tuple-element.4) | data formatting | bytes 3145728
  66.6 0.6 copy.8

commit v4 on v3

--- a/solution.py
+++ b/solution.py
@@ -13,7 +13,7 @@
 B = 48
 PK = 32
 CH = 384
-STEPS = (0, 1, 7, 2, 6, 3, 5, 4)
+STEPS = (0, 1, 7, 2, 4, 3, 5, 6)
 
 
 def dot(a, b):
@@ -53,7 +53,7 @@
 def kernel(
     inputs_hbm, weight_hbm, d_out_hbm, gi, wg_out,
     inputs, weight, d_out, wm, w, acc, g_own, g_other, t_own, t_send, t_other,
-    part, rx, sx, rz, s2, ry, sm, rm,
+    own, part, rx, sx, rz, s2, ry, sm, rm,
     in_sem, wm_s, wm_r, y_s, y_r, z_s, z_r, x_s, x_r, c_s, c_r, t_s, t_r, g_s, g_r,
     rx_s, rx_r, rz_s, rz_r, ry_s, ry_r, rm_s, rm_r,
 ):
@@ -91,10 +91,10 @@
     core_peer = at(y, z, oc)
 
     barrier = pltpu.get_barrier_semaphore()
-    peers = [mp_peer(j) for j in range(1, 8)]
-    peers += [y_peer(d, c) for d in range(1, 8)]
+    peers = [mp_peer(j) for j in (6, 5, 7, 4, 2, 1, 3)]
+    peers += [y_peer(d, c) for d in (4, 3, 5, 2, 6, 1, 7)]
+    peers += [at(y, (z + dz + 8) % 8, c) for dz in (1, -1, 2, -2)]
     peers += [y_peer(d, oc) for d in range(0, 8)]
-    peers += [at(y, (z + dz + 8) % 8, c) for dz in (1, -1, 2, -2)]
     for peer in peers:
         pl.semaphore_signal(barrier, inc=1, device_id=peer, device_id_type=MESH)
     load_w.wait()
@@ -223,6 +223,8 @@
     g_own[:, 256:] = gv
     g_copy = remote(g_own, g_other, g_s, g_r, core_peer)
     g_copy.start()
+    for k in range(4):
+        own[k] = dot(t_own[k], g_own[...])
     t_copy.wait_recv()
     g_copy.wait_recv()
 
@@ -263,7 +265,7 @@
                 ry_copy(k, cc).start()
 
     for k in range(4):
-        p = dot(t_own[k], g_own[...]) + dot(t_other[k], g_other[...])
+        p = own[k] + dot(t_other[k], g_other[...])
         part[k] = p.astype(BF).reshape(4, 2 * B, CH)
         if k < 2:
             to_owner = (2 * c + k - x + 4) % 4
@@ -388,6 +390,21 @@
                 ry_copy(k, cc).wait_send()
 
 
+WRITES = 4
+
+
+def write_out(gi, wg, gi_hbm, wg_hbm, sems):
+    rows = gi.shape[0] // WRITES
+    copies = [pltpu.make_async_copy(wg, wg_hbm, sems.at[WRITES])]
+    for i in range(WRITES):
+        part = pl.ds(i * rows, rows)
+        copies.append(pltpu.make_async_copy(gi.at[part], gi_hbm.at[part], sems.at[i]))
+    for copy in copies:
+        copy.start()
+    for copy in copies:
+        copy.wait()
+
+
 def per_device(inputs, weight, d_out):
     vmem, hbm = pl.BlockSpec(memory_space=pltpu.VMEM), pl.BlockSpec(memory_space=pltpu.HBM)
     dma = pltpu.SemaphoreType.DMA
@@ -395,7 +412,7 @@
     inputs, weight, d_out = (
         pltpu.with_memory_space_constraint(a, pltpu.HBM) for a in (inputs, weight, d_out)
     )
-    return pl.pallas_call(
+    grad_inputs, weight_grad = pl.pallas_call(
         kernel,
         out_shape=(
             jax.ShapeDtypeStruct((tokens, feats), BF),
@@ -415,6 +432,7 @@
             pltpu.VMEM((4, CH, tokens), BF),
             pltpu.VMEM((4, CH, tokens), BF),
             pltpu.VMEM((4, CH, tokens), BF),
+            pltpu.VMEM((4, CH, CH), F32),
             pltpu.VMEM((4, 4, 2 * B, CH), BF),
             pltpu.VMEM((4, 3, 2 * B, CH), BF),
             pltpu.VMEM((3, 2 * B, CH), BF),
@@ -441,6 +459,19 @@
         ),
         name="attention_head_back",
     )(inputs, weight, d_out)
+    anywhere = pl.BlockSpec(memory_space=pl.ANY)
+    return pl.pallas_call(
+        write_out,
+        out_shape=(
+            jax.ShapeDtypeStruct((tokens, feats), BF),
+            jax.ShapeDtypeStruct((B, B), F32),
+        ),
+        in_specs=[anywhere, anywhere],
+        out_specs=(anywhere, anywhere),
+        scratch_shapes=[dma((WRITES + 1,))],
+        compiler_params=pltpu.CompilerParams(vmem_limit_bytes=1 << 20),
+        name="write_out",
+    )(grad_inputs, weight_grad)
 
 
 def solution(mesh):

time: 67.6 us -> 65.8 us (0.973)
  local copies, waits for them, and re-layouts: 1.75 us -> 0 us
    unnamed x2 -> x0, local copies, waits for them, and re-layouts: 1.75 us -> none
    pallas_call x0 -> x1, Pallas kernels: none -> 1.19 us  [per_device(): pl.pallas_call(write_out, out_shape=(jax.ShapeDtypeStruct((tokens, feats)...]
    pallas_call x1, Pallas kernels: 64.8 us -> 63.8 us  [per_device(): pl.pallas_call(kernel, out_shape=(jax.ShapeDtypeStruct((tokens, feats), B...]
where the time goes in v4:
time: 65.8 us; the launch traced here: 65.6 us
  Pallas kernels  65 us (99%)
    pallas_call x1, Pallas kernels, per_device(): pl.pallas_call(kernel, out_shape=(jax.ShapeDtypeStruct((tokens, feats), B...  63.8 us

profile of v4, /device:TPU:1, one launch (start us, length us, event | category | flops | bytes accessed | tf_op | source)
XLA Modules:
  0.0 65.6 jit_solution(2909384356367734006)
XLA Ops:
  0.6 63.8 %attention_head_back.1 = (bf16[256,3072]{1,0:T(8,128)(2,1)S(1)}, f32[48,48]{1,0:T(8,128)S(1)}) custom-call(bf16[256,3072]{1,0:T(8,128)(2,1)} %inputs_hbm.1, bf16[48,48]{1,0:T(8,128)(2,1)} %weight_hbm.1, bf16[256,128]{1,0:T(8,128)(2,1)} %d_out_hbm.1), custom_call_target="tpu_custom_call" | custom-call | tf_op jit(solution)/shard_map/attention_head_back/pallas_call | solution.py:415
  64.4 1.2 %write_out.1 = (bf16[256,3072]{1,0:T(8,128)(2,1)}, f32[48,48]{1,0:T(8,128)}) custom-call(bf16[256,3072]{1,0:T(8,128)(2,1)S(1)} %get-tuple-element.4.gi, f32[48,48]{1,0:T(8,128)S(1)} %get-tuple-element.5.wg), custom_call_target="tpu_custom_call" | custom-call | tf_op jit(solution)/shard_map/write_out/pallas_call | solution.py:463
